TPU v7x, 32 devices: a whole 2x2x4 slice. The times are simulated.
32 devices in a mesh: lat: 4 (over z), lon: 8 (over y, x, core).
Axes of the slice: x: 2, y: 2, z: 4, core: 2. Of those that a mesh axis runs over, the one named last changes fastest.
Arguments:
- grid_tokens: bfloat16 [96, 384, 512], P('lat', 'lon'), may hold values from -28 to 28
- attention_gain: float32 [512], replicated, may hold values from 0.25 to 1.75
- score_weight: bfloat16 [512, 1024], replicated, as said below
- value_weight: bfloat16 [512, 512], replicated, may hold values from -0.25 to 0.25
- output_weight: bfloat16 [512, 512], replicated, may hold values from -0.75 to 0.75
- mixer_gain: float32 [512], replicated, may hold values from 0.25 to 1.75
- first_weight: float32 [2, 8, 64, 64], replicated, may hold values from -0.5 to 0.5
- first_bias: float32 [2, 8, 64], replicated, may hold values from -0.75 to 0.75
- second_weight: float32 [2, 8, 64, 64], replicated, may hold values from -0.5 to 0.5
- second_bias: float32 [2, 8, 64], replicated, may hold values from -0.875 to 0.875
Outputs:
- block_out: bfloat16 [96, 384, 512], P('lat', 'lon')
Inputs may be any that keep to these rules, and one draw needn't show every extreme that they name: `score_weight`: every entry lies within 61 / sqrt(512) of zero.
All inputs are finite; a program needn't handle non-finite values.
Results may differ from a plain program's by a relative error of at most 0.0095.
The roundings to bfloat16 on the way count: a program that leaves them out, or rounds other values in their place, can miss the bound.
Values may be sent and summed in bfloat16 or wider, within the bound.
A program may use at most 192 MiB of HBM per device.

v0:
```python
import functools
import math

import jax
import jax.numpy as jnp
import numpy as np
from jax import lax
from jax.experimental import pallas as pl
from jax.experimental.pallas import tpu as pltpu
from jax.sharding import PartitionSpec as P

HEADS = 8
RADIUS = 6


LANES = 128
CHUNKS = 3
MESH = pl.DeviceIdType.MESH
BLOCK_ROWS = 8
BLOCK_COLS = 16
EDGE = 16


def mixer_tables(total_rows, total_cols, sources, slots):
    kept_rows = total_rows // 2
    kept_cols = total_cols // 4
    modes = kept_cols // sources
    column = np.arange(total_cols)
    angle = 2.0 * np.pi * (np.outer(np.arange(kept_cols), column) % total_cols) / total_cols
    cosine = np.cos(angle).reshape(sources, modes, total_cols)
    sine = np.sin(angle).reshape(sources, modes, total_cols)
    forward = np.zeros((sources, slots, total_cols))
    forward[:, 0 : 2 * modes : 2] = cosine
    forward[:, 1 : 2 * modes : 2] = -sine
    doubled = np.full((kept_cols, 1), 2.0)
    doubled[0] = 1.0
    inverse = (forward.reshape(sources, slots, total_cols)).copy()
    inverse[:, 0 : 2 * modes : 2] *= doubled.reshape(sources, modes, 1)
    inverse[:, 1 : 2 * modes : 2] *= doubled.reshape(sources, modes, 1)
    forward = forward.reshape(sources * slots, total_cols)
    inverse = inverse.reshape(sources * slots, total_cols).T
    frequency = np.arange(kept_rows)
    frequency = frequency + np.where(frequency >= kept_rows // 2, total_rows - kept_rows, 0)
    angle = 2.0 * np.pi * (np.outer(frequency, np.arange(total_rows)) % total_rows) / total_rows
    cosine = np.cos(angle)
    sine = np.sin(angle)
    lat_forward = np.block([[cosine, sine], [-sine, cosine]])
    lat_inverse = np.block([[cosine.T, -sine.T], [sine.T, cosine.T]])
    return tuple(
        np.asarray(table, dtype=jnp.bfloat16)
        for table in (forward, lat_forward, lat_inverse, inverse)
    )


def paired_weights(weight_ref, bias_ref, group, joined, offset):
    size = weight_ref.shape[2]
    blocks = LANES // size
    for index in range(blocks):
        source = group * blocks + index

        def wide(values):
            blank = jnp.zeros_like(values)
            return [values if place == index else blank for place in range(blocks)]

        real = weight_ref[0, source]
        imag = weight_ref[1, source]
        lower = index * size
        joined[lower : lower + size, :] = jnp.concatenate(
            wide(real) + wide(imag), axis=1
        ).astype(jnp.bfloat16)
        lower = LANES + index * size
        joined[lower : lower + size, :] = jnp.concatenate(
            wide(-imag) + wide(real), axis=1
        ).astype(jnp.bfloat16)
    offset[...] = jnp.concatenate(
        [
            bias_ref[part, pl.ds(group * blocks + index, 1), :]
            for part in range(2)
            for index in range(blocks)
        ],
        axis=1,
    )


def block_kernel(
    lat_count,
    lon_count,
    token_ref,
    gain_ref,
    score_ref,
    value_ref,
    output_ref,
    mixer_gain_ref,
    forward_ref,
    lat_forward_ref,
    lat_inverse_ref,
    inverse_ref,
    first_weight_ref,
    first_bias_ref,
    second_weight_ref,
    second_bias_ref,
    after_ref,
    mixer_ref,
    spectral_ref,
    padded,
    query,
    key_value,
    bias,
    columns_in,
    modes_out,
    modes_in,
    modes_work,
    back_out,
    back_in,
    columns_out,
    weight_one,
    bias_one,
    weight_two,
    bias_two,
    send_sem,
    recv_sem,
    own_sem,
    lon_send,
    lon_recv,
    mode_send,
    mode_recv,
    back_send,
    back_recv,
    tile_send,
    tile_recv,
):
    tile_rows, tile_cols, features = token_ref.shape
    total_rows = tile_rows * lat_count
    span = 2 * RADIUS + 1
    head_size = features // HEADS
    pairs = features // LANES
    lat = lax.axis_index("lat")
    lon = lax.axis_index("lon")
    has_upper = lat > 0
    has_lower = lat < lat_count - 1
    left = lax.rem(lon + lon_count - 1, lon_count)
    right = lax.rem(lon + 1, lon_count)

    groups = features // LANES
    parts = lon_count // groups
    sources = lat_count * parts
    part_rows = tile_rows // parts
    chunk_rows = part_rows // CHUNKS
    total_cols = tile_cols * lon_count
    kept_rows = total_rows // 2
    modes = total_cols // 4 // sources
    slots = modes_in.shape[1] // part_rows
    stretch = chunk_rows * slots
    factor = 1.0 / math.sqrt(total_rows * total_cols)
    my_group = lon // parts
    my_part = lax.rem(lon, parts)
    my_source = lat * parts + my_part

    def lon_device(index):
        return (lat, index)

    def mode_device(index):
        return (index // parts, my_group * parts + lax.rem(index, parts))

    send_rows = {-1: (0, RADIUS), 0: (0, tile_rows), 1: (tile_rows - RADIUS, RADIUS)}
    land_rows = {
        -1: (tile_rows + RADIUS, RADIUS),
        0: (RADIUS, tile_rows),
        1: (0, RADIUS),
    }
    send_cols = {-1: (0, EDGE), 0: (0, tile_cols), 1: (tile_cols - EDGE, EDGE)}
    land_cols = {-1: (tile_cols + EDGE, EDGE), 0: (EDGE, tile_cols), 1: (0, EDGE)}
    moves = [(0, -1), (0, 1)] + [(down, across) for down in (-1, 1) for across in (0, -1, 1)]

    def transfer(index):
        down, across = moves[index]
        target = {-1: left, 0: lon, 1: right}[across]
        return pltpu.make_async_remote_copy(
            src_ref=token_ref.at[pl.ds(*send_rows[down]), pl.ds(*send_cols[across]), :],
            dst_ref=padded.at[pl.ds(*land_rows[down]), pl.ds(*land_cols[across]), :],
            send_sem=send_sem.at[index],
            recv_sem=recv_sem.at[index],
            device_id=(lat + down, target),
            device_id_type=MESH,
        )

    barrier = pltpu.get_barrier_semaphore()

    def greet(row):
        for column in (left, lon, right):
            pl.semaphore_signal(
                barrier, inc=1, device_id=(row, column), device_id_type=MESH
            )

    for column in (left, right):
        pl.semaphore_signal(barrier, inc=1, device_id=(lat, column), device_id_type=MESH)

    @pl.loop(1, lon_count)
    def _(step):
        pl.semaphore_signal(
            barrier,
            inc=1,
            device_id=lon_device(lax.rem(lon + step, lon_count)),
            device_id_type=MESH,
        )

    @pl.loop(1, sources)
    def _(step):
        pl.semaphore_signal(
            barrier,
            inc=1,
            device_id=mode_device(lax.rem(my_source + step, sources)),
            device_id_type=MESH,
        )

    @pl.when(has_upper)
    def _():
        greet(lat - 1)

    @pl.when(has_lower)
    def _():
        greet(lat + 1)

    above = (lat + lat_count - 1) // lat_count
    below = (2 * lat_count - 2 - lat) // lat_count
    pl.semaphore_wait(barrier, lon_count + sources + 3 * (above + below))

    for index in (0, 1):
        transfer(index).start()

    @pl.when(has_upper)
    def _():
        for index in (2, 3, 4):
            transfer(index).start()

    @pl.when(has_lower)
    def _():
        for index in (5, 6, 7):
            transfer(index).start()

    own = pltpu.make_async_copy(
        token_ref,
        padded.at[pl.ds(RADIUS, tile_rows), pl.ds(EDGE, tile_cols), :],
        own_sem,
    )
    own.start()
    blank = jnp.zeros((RADIUS, tile_cols + 2 * EDGE, features), jnp.bfloat16)

    @pl.when(jnp.logical_not(has_upper))
    def _():
        padded[:RADIUS] = blank

    @pl.when(jnp.logical_not(has_lower))
    def _():
        padded[tile_rows + RADIUS :] = blank

    def norm(data, gain):
        centre = jnp.mean(data, axis=-1, keepdims=True)
        centred = data - centre
        spread = jnp.mean(centred * centred, axis=-1, keepdims=True)
        return (centred * lax.rsqrt(spread + 1e-05) * gain).astype(jnp.bfloat16)

    def spread_pairs(ref, base, rows, values, cols):
        shaped = values.astype(jnp.bfloat16).reshape(RADIUS, cols, values.shape[1])
        for pair in range(values.shape[1] // LANES):
            ref[base + pair, rows] = shaped[:, :, pair * LANES : (pair + 1) * LANES]

    scale = 1.0 / math.sqrt(head_size)

    @pl.loop(0, tile_rows // RADIUS)
    def _(step):
        rows = pl.ds(step * RADIUS, RADIUS)
        data = token_ref[rows].astype(jnp.float32).reshape(-1, features)
        inputs = norm(data, gain_ref[...])
        values = jnp.dot(inputs, score_ref[:, :features], preferred_element_type=jnp.float32)
        values = values.astype(jnp.bfloat16).astype(jnp.float32) * scale
        spread_pairs(query, 0, rows, values, tile_cols)

    paired_weights(first_weight_ref, first_bias_ref, my_group, weight_one, bias_one)
    paired_weights(second_weight_ref, second_bias_ref, my_group, weight_two, bias_two)
    own.wait()
    for index in (0, 1):
        transfer(index).wait()

    @pl.when(has_lower)
    def _():
        for index in (2, 3, 4):
            transfer(index).wait_recv()

    @pl.when(has_upper)
    def _():
        for index in (5, 6, 7):
            transfer(index).wait_recv()

    near = EDGE // 2
    wide = tile_cols + 2 * near

    @pl.loop(0, tile_rows // RADIUS + 2)
    def _(step):
        rows = pl.ds(step * RADIUS, RADIUS)
        data = padded[rows].astype(jnp.float32)[:, near : near + wide, :].reshape(-1, features)
        inputs = norm(data, gain_ref[...])
        keys = jnp.dot(inputs, score_ref[:, features:], preferred_element_type=jnp.float32)
        spread_pairs(key_value, 0, rows, keys, wide)
        values = jnp.dot(inputs, value_ref[...], preferred_element_type=jnp.float32)
        spread_pairs(key_value, pairs, rows, values, wide)

    block = BLOCK_ROWS * BLOCK_COLS
    key_rows = BLOCK_ROWS + 2 * RADIUS
    key_cols = BLOCK_COLS + 2 * near
    reach = key_rows * key_cols
    col_blocks = tile_cols // BLOCK_COLS

    def attend(row, col):
        lower_lane = lax.broadcasted_iota(jnp.int32, (block, LANES), 1) < head_size
        heads = []
        for pair in range(pairs):
            asked = query[pair, pl.ds(row, BLOCK_ROWS), pl.ds(col, BLOCK_COLS), :]
            asked = asked.reshape(block, LANES).astype(jnp.float32)
            asked = jnp.concatenate(
                [jnp.where(lower_lane, asked, 0.0), jnp.where(lower_lane, 0.0, asked)], axis=0
            ).astype(jnp.bfloat16)
            window = (pl.ds(row, key_rows), pl.ds(col, key_cols), slice(None))
            keys = key_value[(pair, *window)].reshape(reach, LANES)
            values = key_value[(pairs + pair, *window)].reshape(reach, LANES)
            scores = lax.dot_general(
                asked, keys, (((1,), (1,)), ((), ())), preferred_element_type=jnp.float32
            )
            scores = (scores.reshape(2, block, reach) + bias[...]).reshape(2 * block, reach)
            weights = jnp.exp(scores - jnp.max(scores, axis=1, keepdims=True))
            total = jnp.sum(weights, axis=1, keepdims=True)
            mixed = jnp.dot(
                weights.astype(jnp.bfloat16), values, preferred_element_type=jnp.float32
            )
            mixed = mixed / total
            heads.append(jnp.where(lower_lane, mixed[:block], mixed[block:]))
        attended = jnp.concatenate(heads, axis=1).astype(jnp.bfloat16)
        place = (pl.ds(row, BLOCK_ROWS), pl.ds(col, BLOCK_COLS), slice(None))
        after = token_ref[place].astype(jnp.float32).reshape(block, features)
        after = after + jnp.dot(attended, output_ref[...], preferred_element_type=jnp.float32)
        after = after.astype(jnp.bfloat16)
        shape = (BLOCK_ROWS, BLOCK_COLS, features)
        after_ref[place] = after.reshape(shape)
        mixer_ref[place] = norm(after.astype(jnp.float32), mixer_gain_ref[...]).reshape(shape)

    def lon_piece(chunk, owner):
        group = owner // parts
        part = lax.rem(owner, parts)
        return mixer_ref.at[
            pl.ds(part * part_rows + chunk * chunk_rows, chunk_rows),
            :,
            pl.ds(pl.multiple_of(group * LANES, LANES), LANES),
        ]

    def column_piece(ref, chunk, owner):
        return ref.at[
            pl.ds(chunk * chunk_rows, chunk_rows),
            pl.ds(pl.multiple_of(owner * tile_cols, 16), tile_cols),
            :,
        ]

    def mode_piece(ref, chunk, owner):
        return ref.at[owner, pl.ds(chunk * stretch, stretch), :]

    def tile_piece(chunk, owner):
        group = owner // parts
        part = lax.rem(owner, parts)
        return spectral_ref.at[
            pl.ds(part * part_rows + chunk * chunk_rows, chunk_rows),
            :,
            pl.ds(pl.multiple_of(group * LANES, LANES), LANES),
        ]

    def send_all(chunk, count, mine, device, source, target, send_sem, recv_sem):
        pltpu.make_async_copy(source(mine), target(mine), recv_sem.at[chunk, mine]).start()

        @pl.loop(1, count)
        def _(step):
            peer = lax.rem(mine + step, count)
            pltpu.make_async_remote_copy(
                src_ref=source(peer),
                dst_ref=target(mine),
                send_sem=send_sem.at[chunk, peer],
                recv_sem=recv_sem.at[chunk, mine],
                device_id=device(peer),
                device_id_type=MESH,
            ).start()

    def wait_all(chunk, count, mine, device, source, target, send_sem, recv_sem):
        pltpu.make_async_copy(source(mine), target(mine), recv_sem.at[chunk, mine]).wait()

        @pl.loop(1, count)
        def _(step):
            peer = lax.rem(mine + step, count)
            pltpu.make_async_remote_copy(
                src_ref=source(peer),
                dst_ref=target(peer),
                send_sem=send_sem.at[chunk, peer],
                recv_sem=recv_sem.at[chunk, peer],
                device_id=device(peer),
                device_id_type=MESH,
            ).wait_recv()

    def wait_sent(chunk, count, mine, device, source, target, send_sem, recv_sem):
        @pl.loop(1, count)
        def _(step):
            peer = lax.rem(mine + step, count)
            pltpu.make_async_remote_copy(
                src_ref=source(peer),
                dst_ref=target(peer),
                send_sem=send_sem.at[chunk, peer],
                recv_sem=recv_sem.at[chunk, peer],
                device_id=device(peer),
                device_id_type=MESH,
            ).wait_send()

    def lon_plan(chunk):
        return (
            chunk,
            lon_count,
            lon,
            lon_device,
            lambda owner: lon_piece(chunk, owner),
            lambda owner: column_piece(columns_in, chunk, owner),
            lon_send,
            lon_recv,
        )

    def mode_plan(chunk):
        return (
            chunk,
            sources,
            my_source,
            mode_device,
            lambda owner: mode_piece(modes_out, chunk, owner),
            lambda owner: mode_piece(modes_in, chunk, owner),
            mode_send,
            mode_recv,
        )

    def back_plan(chunk):
        return (
            chunk,
            sources,
            my_source,
            mode_device,
            lambda owner: mode_piece(back_out, chunk, owner),
            lambda owner: mode_piece(back_in, chunk, owner),
            back_send,
            back_recv,
        )

    def tile_plan(chunk):
        return (
            chunk,
            lon_count,
            lon,
            lon_device,
            lambda owner: column_piece(columns_out, chunk, owner),
            lambda owner: tile_piece(chunk, owner),
            tile_send,
            tile_recv,
        )

    def send_rows_along(part, chunk):
        for group in range(groups):
            peer = group * parts + part
            source = lon_piece(chunk, peer)
            target = column_piece(columns_in, chunk, lon)

            @pl.when(peer == lon)
            def _():
                pltpu.make_async_copy(source, target, lon_recv.at[chunk, lon]).start()

            @pl.when(peer != lon)
            def _():
                pltpu.make_async_remote_copy(
                    src_ref=source,
                    dst_ref=target,
                    send_sem=lon_send.at[chunk, peer],
                    recv_sem=lon_recv.at[chunk, lon],
                    device_id=lon_device(peer),
                    device_id_type=MESH,
                ).start()

    @pl.loop(0, tile_rows // BLOCK_ROWS)
    def _(row_block):
        row = row_block * BLOCK_ROWS
        token = lax.broadcasted_iota(jnp.int32, (block, reach), 0)
        other = lax.broadcasted_iota(jnp.int32, (block, reach), 1)
        top = lat * tile_rows + row
        start = jnp.clip(top + token // BLOCK_COLS - RADIUS, 0, total_rows - span)
        down = top - RADIUS + other // key_cols - start
        across = other % key_cols - near - token % BLOCK_COLS
        inside = (down >= 0) & (down < span) & (across >= -RADIUS) & (across <= RADIUS)
        bias[...] = jnp.where(inside, 0.0, -1e30)

        @pl.loop(0, col_blocks)
        def _(col_block):
            attend(row, pl.multiple_of(col_block * BLOCK_COLS, BLOCK_COLS))

        for index in range(BLOCK_ROWS // chunk_rows):
            ready = row_block * (BLOCK_ROWS // chunk_rows) + index
            send_rows_along(ready // CHUNKS, lax.rem(ready, CHUNKS))

    for chunk in range(CHUNKS):
        wait_all(*lon_plan(chunk))
        first = chunk * chunk_rows
        field = jnp.concatenate([columns_in[first + row] for row in range(chunk_rows)], axis=1)
        along = jnp.dot(forward_ref[...], field, preferred_element_type=jnp.float32)
        along = jnp.concatenate(
            [
                along[:, row * LANES : (row + 1) * LANES].reshape(sources, slots, LANES)
                for row in range(chunk_rows)
            ],
            axis=1,
        )
        modes_out[:, chunk * stretch : (chunk + 1) * stretch, :] = along.astype(jnp.bfloat16)
        send_all(*mode_plan(chunk))
    for chunk in range(CHUNKS):
        wait_all(*mode_plan(chunk))
    modes_work[...] = modes_in[...].astype(jnp.float32).reshape(modes_work.shape)

    batch = 4 if modes % 4 == 0 else modes
    for start in range(0, modes, batch):
        members = range(start, start + batch)

        def every_row(slot):
            return modes_work[pl.ds(slot, total_rows, stride=slots), :].astype(jnp.bfloat16)

        field = jnp.concatenate(
            [
                jnp.concatenate([every_row(2 * mode), every_row(2 * mode + 1)], axis=0)
                for mode in members
            ],
            axis=1,
        )
        spectrum = (
            jnp.dot(lat_forward_ref[...], field, preferred_element_type=jnp.float32) * factor
        )
        spectrum = jnp.concatenate(
            [
                jnp.concatenate(
                    [
                        spectrum[:kept_rows, index * LANES : (index + 1) * LANES],
                        spectrum[kept_rows:, index * LANES : (index + 1) * LANES],
                    ],
                    axis=1,
                )
                for index in range(batch)
            ],
            axis=0,
        ).astype(jnp.bfloat16)
        hidden = jnp.dot(spectrum, weight_one[...], preferred_element_type=jnp.float32)
        hidden = jnp.maximum(hidden + bias_one[...], 0.0).astype(jnp.bfloat16)
        filtered = jnp.dot(hidden, weight_two[...], preferred_element_type=jnp.float32)
        filtered = filtered + bias_two[...]
        filtered = jnp.concatenate(
            [
                jnp.concatenate(
                    [
                        filtered[index * kept_rows : (index + 1) * kept_rows, :LANES],
                        filtered[index * kept_rows : (index + 1) * kept_rows, LANES:],
                    ],
                    axis=0,
                )
                for index in range(batch)
            ],
            axis=1,
        ).astype(jnp.bfloat16)
        rows = jnp.dot(lat_inverse_ref[...], filtered, preferred_element_type=jnp.float32)
        for index, mode in enumerate(members):
            lanes = slice(index * LANES, (index + 1) * LANES)
            modes_work[pl.ds(2 * mode, total_rows, stride=slots), :] = rows[:total_rows, lanes]
            modes_work[pl.ds(2 * mode + 1, total_rows, stride=slots), :] = rows[total_rows:, lanes]
    back_out[...] = modes_work[...].reshape(back_out.shape).astype(jnp.bfloat16)
    for chunk in range(CHUNKS):
        send_all(*back_plan(chunk))
    for chunk in range(CHUNKS):
        wait_all(*back_plan(chunk))
        first = chunk * chunk_rows
        piece = back_in[:, chunk * stretch : (chunk + 1) * stretch, :].astype(jnp.float32)
        field = jnp.concatenate(
            [
                piece[:, row * slots : (row + 1) * slots, :].reshape(sources * slots, LANES)
                for row in range(chunk_rows)
            ],
            axis=1,
        ).astype(jnp.bfloat16)
        whole = jnp.dot(inverse_ref[...], field, preferred_element_type=jnp.float32) * factor
        for row in range(chunk_rows):
            columns_out[first + row] = whole[:, row * LANES : (row + 1) * LANES].astype(
                jnp.bfloat16
            )
        send_all(*tile_plan(chunk))
    for chunk in range(CHUNKS):
        wait_all(*tile_plan(chunk))
    for chunk in range(CHUNKS):
        for plan in (lon_plan, mode_plan, back_plan, tile_plan):
            wait_sent(*plan(chunk))

    @pl.when(has_upper)
    def _():
        for index in (2, 3, 4):
            transfer(index).wait_send()

    @pl.when(has_lower)
    def _():
        for index in (5, 6, 7):
            transfer(index).wait_send()


def shards(
    grid_tokens,
    attention_gain,
    score_weight,
    value_weight,
    output_weight,
    mixer_gain,
    first_weight,
    first_bias,
    second_weight,
    second_bias,
):
    tile_rows, tile_cols, features = grid_tokens.shape
    lat_count = lax.axis_size("lat")
    lon_count = lax.axis_size("lon")
    pairs = features // LANES
    parts = lon_count // pairs
    sources = lat_count * parts
    part_rows = tile_rows // parts
    total_rows = tile_rows * lat_count
    total_cols = tile_cols * lon_count
    modes = total_cols // 4 // sources
    slots = -(-2 * modes // 8) * 8
    tables = mixer_tables(total_rows, total_cols, sources, slots)
    padded_rows = tile_rows + 2 * RADIUS
    block = BLOCK_ROWS * BLOCK_COLS
    reach = (BLOCK_ROWS + 2 * RADIUS) * (BLOCK_COLS + EDGE)
    vmem = pl.BlockSpec(memory_space=pltpu.VMEM)
    shape = jax.ShapeDtypeStruct(grid_tokens.shape, jnp.bfloat16)
    modes_shape = (sources, part_rows * slots, LANES)
    after_attention, mixer_in, spectral = pl.pallas_call(
        functools.partial(block_kernel, lat_count, lon_count),
        out_shape=(shape, shape, shape),
        in_specs=[vmem] * 14,
        out_specs=(vmem, vmem, vmem),
        scratch_shapes=[
            pltpu.VMEM((padded_rows, tile_cols + 2 * EDGE, features), jnp.bfloat16),
            pltpu.VMEM((pairs, tile_rows, tile_cols, LANES), jnp.bfloat16),
            pltpu.VMEM((2 * pairs, padded_rows, tile_cols + EDGE, LANES), jnp.bfloat16),
            pltpu.VMEM((block, reach), jnp.float32),
            pltpu.VMEM((part_rows, total_cols, LANES), jnp.bfloat16),
            pltpu.VMEM(modes_shape, jnp.bfloat16),
            pltpu.VMEM(modes_shape, jnp.bfloat16),
            pltpu.VMEM((sources * part_rows * slots, LANES), jnp.float32),
            pltpu.VMEM(modes_shape, jnp.bfloat16),
            pltpu.VMEM(modes_shape, jnp.bfloat16),
            pltpu.VMEM((part_rows, total_cols, LANES), jnp.bfloat16),
            pltpu.VMEM((2 * LANES, 2 * LANES), jnp.bfloat16),
            pltpu.VMEM((1, 2 * LANES), jnp.float32),
            pltpu.VMEM((2 * LANES, 2 * LANES), jnp.bfloat16),
            pltpu.VMEM((1, 2 * LANES), jnp.float32),
            pltpu.SemaphoreType.DMA((8,)),
            pltpu.SemaphoreType.DMA((8,)),
            pltpu.SemaphoreType.DMA,
        ]
        + [
            pltpu.SemaphoreType.DMA((CHUNKS, count))
            for count in (lon_count, sources, sources, lon_count)
            for _ in range(2)
        ],
        compiler_params=pltpu.CompilerParams(
            collective_id=1, has_side_effects=True, vmem_limit_bytes=56 * 1024 * 1024
        ),
        name="mixed_block",
    )(
        grid_tokens,
        attention_gain.reshape(1, features),
        score_weight,
        value_weight,
        output_weight,
        mixer_gain.reshape(1, features),
        *tables,
        first_weight,
        first_bias,
        second_weight,
        second_bias,
    )
    summed = (
        after_attention.astype(jnp.float32)
        + mixer_in.astype(jnp.float32)
        + spectral.astype(jnp.float32)
    )
    return summed.astype(jnp.bfloat16)


def solution(mesh):
    placed = (P("lat", "lon", None), P(), P(), P(), P(), P(), P(), P(), P(), P())
    return jax.shard_map(
        shards, mesh=mesh, in_specs=placed, out_specs=P("lat", "lon", None), check_vma=False
    )
```

profile of v0, /device:TPU:0, one launch (start us, length us, event | category | flops | bytes accessed | tf_op | source)
XLA Modules:
  0.0 90.0 jit_solution(13745345765154618083)
XLA Ops:
  0.0 86.4 %mixed_block.1 = (bf16[24,48,512]{2,1,0:T(8,128)(2,1)}, bf16[24,48,512]{2,1,0:T(8,128)(2,1)}, bf16[24,48,512]{2,1,0:T(8,128)(2,1)}) custom-call(bf16[24,48,512]{2,1,0:T(8,128)(2,1)} %token_ref.1, f32[1,512]{1,0:T(1,128)} %bitcast.2, bf16[512,1024]{1,0:T(8,128)(2,1)} %score_ref.1, bf16[512,512]{1,0:T(8,128)(2,1)} %value_ref.1, bf16[512,512]{1,0:T(8,128)(2,1)} %output_ref.1, ...), custom_call_target="tpu_custom_call" | custom-call | tf_op jit(solution)/shard_map/mixed_block/pallas_call | solution.py:643
  86.5 3.6 %add_convert_fusion = bf16[24,48,512]{2,1,0:T(8,128)(2,1)} fusion(bf16[24,48,512]{2,1,0:T(8,128)(2,1)} %get-tuple-element.10, bf16[24,48,512]{2,1,0:T(8,128)(2,1)} %get-tuple-element.9, bf16[24,48,512]{2,1,0:T(8,128)(2,1)} %get-tuple-element.8), kind=kLoop, calls=%fused_computation | loop fusion | flops 3538944 | bytes 4718592 | tf_op jit(solution)/shard_map/convert_element_type | solution.py:695
where the time goes:
time: 91.5 us; the launch traced here: 90 us
  Pallas kernels  86.4 us (94%)
  other arithmetic  3.59 us (4%)
    pallas_call x1, Pallas kernels, shards(): pl.pallas_call(functools.partial(block_kernel, lat_count, lon_count), out...  86.4 us
    convert_element_type x1, other arithmetic, shards(): return summed.astype(jnp.bfloat16)  3.59 us

commit v1 on v0

--- a/solution.py
+++ b/solution.py
@@ -99,6 +99,7 @@
     first_bias_ref,
     second_weight_ref,
     second_bias_ref,
+    sum_ref,
     after_ref,
     mixer_ref,
     spectral_ref,
@@ -595,6 +596,12 @@
         send_all(*tile_plan(chunk))
     for chunk in range(CHUNKS):
         wait_all(*tile_plan(chunk))
+        for part in range(parts):
+            first = part * part_rows + chunk * chunk_rows
+            rows = slice(first, first + chunk_rows)
+            summed = after_ref[rows].astype(jnp.float32) + mixer_ref[rows].astype(jnp.float32)
+            summed = summed + spectral_ref[rows].astype(jnp.float32)
+            sum_ref[rows] = summed.astype(jnp.bfloat16)
     for chunk in range(CHUNKS):
         for plan in (lon_plan, mode_plan, back_plan, tile_plan):
             wait_sent(*plan(chunk))
@@ -640,12 +647,13 @@
     vmem = pl.BlockSpec(memory_space=pltpu.VMEM)
     shape = jax.ShapeDtypeStruct(grid_tokens.shape, jnp.bfloat16)
     modes_shape = (sources, part_rows * slots, LANES)
-    after_attention, mixer_in, spectral = pl.pallas_call(
+    return pl.pallas_call(
         functools.partial(block_kernel, lat_count, lon_count),
-        out_shape=(shape, shape, shape),
+        out_shape=shape,
         in_specs=[vmem] * 14,
-        out_specs=(vmem, vmem, vmem),
-        scratch_shapes=[
+        out_specs=vmem,
+        scratch_shapes=[pltpu.VMEM(grid_tokens.shape, jnp.bfloat16) for _ in range(3)]
+        + [
             pltpu.VMEM((padded_rows, tile_cols + 2 * EDGE, features), jnp.bfloat16),
             pltpu.VMEM((pairs, tile_rows, tile_cols, LANES), jnp.bfloat16),
             pltpu.VMEM((2 * pairs, padded_rows, tile_cols + EDGE, LANES), jnp.bfloat16),
@@ -687,12 +695,6 @@
         second_weight,
         second_bias,
     )
-    summed = (
-        after_attention.astype(jnp.float32)
-        + mixer_in.astype(jnp.float32)
-        + spectral.astype(jnp.float32)
-    )
-    return summed.astype(jnp.bfloat16)
 
 
 def solution(mesh):

time: 91.5 us -> 89.7 us (0.980)
  other arithmetic: 3.59 us -> 0 us
  local copies, waits for them, and re-layouts: 0 us -> 2.36 us
    convert_element_type x1 -> x0, other arithmetic: 3.59 us -> none  [shards(): return summed.astype(jnp.bfloat16)]
    unnamed x0 -> x1, local copies, waits for them, and re-layouts: none -> 2.36 us
where the time goes in v1:
time: 89.7 us; the launch traced here: 88 us
  Pallas kernels  85.6 us (95%)
  local copies, waits for them, and re-layouts  2.36 us (3%)
    pallas_call x1, Pallas kernels, shards(): pl.pallas_call(functools.partial(block_kernel, lat_count, lon_count), out...  85.6 us
    unnamed x1, local copies, waits for them, and re-layouts  2.36 us

profile of v1, /device:TPU:0, one launch (start us, length us, event | category | flops | bytes accessed | tf_op | source)
XLA Modules:
  0.0 88.0 jit_solution(192444577633993301)
XLA Ops:
  0.0 85.6 %mixed_block.1 = bf16[24,48,512]{2,1,0:T(8,128)(2,1)} custom-call(bf16[24,48,512]{2,1,0:T(8,128)(2,1)} %token_ref.1, f32[1,512]{1,0:T(1,128)} %bitcast.2, bf16[512,1024]{1,0:T(8,128)(2,1)} %score_ref.1, bf16[512,512]{1,0:T(8,128)(2,1)} %value_ref.1, bf16[512,512]{1,0:T(8,128)(2,1)} %output_ref.1, f32[1,512]{1,0:T(1,128)} %bitcast.3, ...), custom_call_target="tpu_custom_call" | custom-call | tf_op jit(solution)/shard_map/mixed_block/pallas_call | solution.py:650
  85.7 2.4 %copy.16 = bf16[24,48,512]{2,1,0:T(8,128)(2,1)} copy(bf16[24,48,512]{2,1,0:T(8,128)(2,1)} %mixed_block.1) | data formatting | bytes 2359296
